TPU v7x, 32 devices: a whole 2x2x4 slice. The times are simulated.
32 devices in a mesh: dp: 16 (over z, x, core), tensor: 2 (over y).
Axes of the slice: x: 2, y: 2, z: 4, core: 2. Of those that a mesh axis runs over, the one named last changes fastest.
Arguments:
- clips: bfloat16 [16, 8, 8, 16, 1024], P('dp', None, None, None, 'tensor'), may hold values from -6 to 6
- out_grad: bfloat16 [16, 8, 8, 16, 1024], P('dp', None, None, None, 'tensor'), may hold values from -6 to 6
- spatial_weight: bfloat16 [3, 3, 1024, 1024], P(None, None, None, 'tensor'), may hold values from -0.0625 to 0.0625
- temporal_weight: bfloat16 [3, 1024, 1024], P(None, 'tensor'), may hold values from -0.109375 to 0.109375
Outputs:
- mixed: bfloat16 [16, 8, 8, 16, 1024], P('dp', None, None, None, 'tensor')
- clip_grad: bfloat16 [16, 8, 8, 16, 1024], P('dp', None, None, None, 'tensor')
- spatial_grad: bfloat16 [3, 3, 1024, 1024], P(None, None, 'dp', 'tensor')
- temporal_grad: bfloat16 [3, 1024, 1024], P(None, 'tensor', 'dp')
All inputs are finite; a program needn't handle non-finite values.
Results may differ from a plain program's by a relative error of at most 0.006.
Values may be sent and summed in bfloat16 or wider, within the bound.
A program may use at most 128 MiB of HBM per device.

v0:
```python
import jax
import jax.numpy as jnp
from jax import lax
from jax.sharding import PartitionSpec as P

GS = 32


def group_silu(values):
    shaped = values.reshape(values.shape[0], -1, values.shape[-1] // GS, GS)
    center = jnp.mean(shaped, axis=(1, 3), keepdims=True)
    offsets = shaped - center
    spread = jnp.mean(offsets * offsets, axis=(1, 3), keepdims=True)
    return jax.nn.silu(offsets * lax.rsqrt(spread + 1e-05)).reshape(values.shape)


def spatial_conv(inputs, kernel):
    dims = inputs.shape
    flat = inputs.reshape((dims[0] * dims[1], dims[2], dims[3], dims[4]))
    result = lax.conv_general_dilated(
        flat,
        kernel,
        (1, 1),
        ((1, 1), (1, 1)),
        dimension_numbers=("NHWC", "HWIO", "NHWC"),
        preferred_element_type=jnp.float32,
    )
    return result.reshape(dims[:4] + (kernel.shape[3],))


def flipped(kernel):
    return jnp.transpose(kernel[::-1, ::-1], (0, 1, 3, 2))


def spatial_wgrad(inputs, grads):
    dims = inputs.shape
    padded = jnp.pad(inputs, ((0, 0), (0, 0), (1, 1), (1, 1), (0, 0)))
    right_side = grads.reshape(-1, grads.shape[-1])
    collected = []
    for row_tap in range(3):
        for col_tap in range(3):
            window = padded[:, :, row_tap : row_tap + dims[2], col_tap : col_tap + dims[3]].reshape(
                -1, dims[4]
            )
            collected.append(
                lax.dot_general(
                    window, right_side, (((0,), (0,)), ((), ())), preferred_element_type=jnp.float32
                )
            )
    return jnp.stack(collected).reshape(3, 3, dims[4], grads.shape[-1])


def temporal_conv(inputs, kernel):
    frame_count = inputs.shape[1]
    padded = jnp.pad(inputs, ((0, 0), (1, 1), (0, 0), (0, 0), (0, 0)))
    result = jnp.zeros((inputs.size // inputs.shape[-1], kernel.shape[2]), jnp.float32)
    for kernel_tap in range(3):
        window = padded[:, kernel_tap : kernel_tap + frame_count].reshape(-1, inputs.shape[-1])
        result = result + jnp.dot(window, kernel[kernel_tap], preferred_element_type=jnp.float32)
    return result.reshape(inputs.shape[:4] + (kernel.shape[2],))


def temporal_back(grads, kernel):
    frame_count = grads.shape[1]
    padded = jnp.pad(grads, ((0, 0), (1, 1), (0, 0), (0, 0), (0, 0)))
    result = jnp.zeros((grads.size // grads.shape[-1], kernel.shape[1]), jnp.float32)
    for kernel_tap in range(3):
        window = padded[:, 2 - kernel_tap : 2 - kernel_tap + frame_count].reshape(
            -1, grads.shape[-1]
        )
        result = result + lax.dot_general(
            window, kernel[kernel_tap], (((1,), (1,)), ((), ())), preferred_element_type=jnp.float32
        )
    return result.reshape(grads.shape[:4] + (kernel.shape[1],))


def temporal_wgrad(inputs, grads):
    frame_count = inputs.shape[1]
    padded = jnp.pad(inputs, ((0, 0), (1, 1), (0, 0), (0, 0), (0, 0)))
    right_side = grads.reshape(-1, grads.shape[-1])
    collected = []
    for kernel_tap in range(3):
        window = padded[:, kernel_tap : kernel_tap + frame_count].reshape(-1, inputs.shape[-1])
        collected.append(
            lax.dot_general(
                window, right_side, (((0,), (0,)), ((), ())), preferred_element_type=jnp.float32
            )
        )
    return jnp.stack(collected)


def per_device(clips, out_grad, spatial_weight, temporal_weight):
    position_count = (
        clips.shape[0] * clips.shape[1] * clips.shape[2] * clips.shape[3] * lax.axis_size("dp")
    )
    grad_scale = 1.0 / jnp.sqrt(jnp.float32(position_count))
    first_act, pull_first = jax.vjp(group_silu, clips.astype(jnp.float32))
    hidden_first = first_act.astype(jnp.bfloat16)
    first_full = lax.all_gather(hidden_first, "tensor", axis=4, tiled=True)
    spatial_out = spatial_conv(first_full, spatial_weight)
    second_act, pull_second = jax.vjp(group_silu, spatial_out)
    hidden_second = second_act.astype(jnp.bfloat16)
    temporal_out = lax.psum_scatter(
        temporal_conv(hidden_second, temporal_weight), "tensor", scatter_dimension=4, tiled=True
    )
    mixed = (clips.astype(jnp.float32) + temporal_out).astype(jnp.bfloat16)
    grad_full = lax.all_gather(out_grad, "tensor", axis=4, tiled=True)
    grad_second = temporal_back(grad_full, temporal_weight)
    grad_spatial = pull_second(grad_second)[0].astype(jnp.bfloat16)
    temporal_local = temporal_wgrad(hidden_second, grad_full)
    grad_partial = spatial_conv(grad_spatial, flipped(spatial_weight))
    grad_first = lax.psum_scatter(grad_partial, "tensor", scatter_dimension=4, tiled=True)
    spatial_local = spatial_wgrad(first_full, grad_spatial)
    spatial_share, temporal_share = (
        lax.psum_scatter(spatial_local, "dp", scatter_dimension=2, tiled=True),
        lax.psum_scatter(temporal_local, "dp", scatter_dimension=2, tiled=True),
    )
    clip_grad = (out_grad.astype(jnp.float32) + pull_first(grad_first)[0]).astype(jnp.bfloat16)
    spatial_out_grad = (spatial_share * grad_scale).astype(jnp.bfloat16)
    temporal_out_grad = (temporal_share * grad_scale).astype(jnp.bfloat16)
    return (mixed, clip_grad, spatial_out_grad, temporal_out_grad)


def solution(mesh):
    placed = (
        P("dp", None, None, None, "tensor"),
        P("dp", None, None, None, "tensor"),
        P(None, None, None, "tensor"),
        P(None, "tensor", None),
    )
    return jax.shard_map(
        per_device,
        mesh=mesh,
        in_specs=placed,
        out_specs=(
            P("dp", None, None, None, "tensor"),
            P("dp", None, None, None, "tensor"),
            P(None, None, "dp", "tensor"),
            P(None, "tensor", "dp"),
        ),
        check_vma=False,
    )
```

profile of v0, /device:TPU:0, one launch (start us, length us, event | category | flops | bytes accessed | tf_op | source)
XLA Modules:
  0.0 631.4 jit_solution(9699012342714584490)
XLA Ops:
  7.2 1.9 convert_reduce_fusion
  9.5 2.1 fusion.13
  12.5 2.1 fusion.10
  14.7 1.6 copy.103
  16.3 34.2 %all-gather.3.cloned.1.call-done = bf16[1,8,8,16,1024]{4,1,3,2,0:T(8,128)(2,1)} async-done(((bf16[1,8,8,16,512]{4,1,3,2,0:T(8,128)(2,1)}), bf16[1,8,8,16,1024]{4,1,3,2,0:T(8,128)(2,1)}) %all-gather.3.cloned.1.call-update) | async-done | bytes 2097168 | tf_op jit(solution)/shard_map/all_gather | solution.py:99
  50.6 13.6 %fusion.116 = (f32[512]{0:T(512)S(1)}, f32[8,8,16,512]{3,0,2,1:T(8,128)S(1)}) fusion(bf16[3,3,1024,512]{3,2,1,0:T(8,128)(2,1)} %param.6, bf16[1,8,8,16,1024]{4,1,3,2,0:T(8,128)(2,1)} %all-gather.3.cloned.1.call-done), kind=kOutput, calls=%fused_computation.133 | convolution fusion | flops 8489795072 | bytes 13633536 | tf_op jit(solution)/shard_map/conv_general_dilated | solution.py:20
  64.6 2.6 copy.110
  67.8 18.1 %all-gather.5.cloned.1.call-done = bf16[1,8,8,16,1024]{4,1,3,2,0:T(8,128)(2,1)} async-done(((bf16[1,8,8,16,512]{4,1,3,2,0:T(8,128)(2,1)}), bf16[1,8,8,16,1024]{4,1,3,2,0:T(8,128)(2,1)}) %all-gather.5.cloned.1.call-update) | async-done | bytes 2097168 | tf_op jit(solution)/shard_map/all_gather | solution.py:107
  85.8 3.4 pad_slice_fusion
  99.0 14.7 %multiply_reduce_fusion = f32[512]{0:T(512)S(1)} fusion(f32[8,8,16,512]{3,0,2,1:T(8,128)S(1)} %get-tuple-element.35, f32[512]{0:T(512)S(1)} %sub.79, f32[512]{0:T(512)S(1)} %mul.269, f32[8,8,16,512]{3,2,1,0:T(8,128)S(1)} %bitcast.191), kind=kLoop, calls=%fused_computation.85 | loop fusion | flops 6815232 | bytes 4200448 | tf_op jit(solution)/shard_map/transpose(jvp())/reduce_sum | solution.py:14
  114.2 3.4 fusion.23
  117.9 4.9 fusion.19
  126.8 3.2 pad_maximum_fusion
  130.0 9.4 %copy.111 = f32[3,512,1024]{1,0,2:T(4,128)} copy(f32[3,512,1024]{2,1,0:T(8,128)} %pad_maximum_fusion) | data formatting | bytes 12582912 | tf_op jit(solution)/shard_map/stack | solution.py:89
  140.6 13.9 %convolution_bitcast_fusion = f32[1,8,8,16,1024]{4,1,3,2,0:T(8,128)} fusion(bf16[8,8,16,512]{3,0,2,1:T(8,128)(2,1)S(1)} %copy-done.8, bf16[3,3,1024,512]{3,2,1,0:T(8,128)(2,1)} %param.6), kind=kOutput, calls=%fused_computation.30 | convolution fusion | flops 8489271296 | bytes 14680064 | tf_op jit(solution)/shard_map/conv_general_dilated | solution.py:20
  161.1 4.3 copy.102
  167.0 2.6 bitcast_dynamic-update-slice_fusion.8
  169.7 2.6 bitcast_dynamic-update-slice_fusion.7
  172.3 2.6 bitcast_dynamic-update-slice_fusion.6
  174.9 2.6 bitcast_dynamic-update-slice_fusion.5
  177.5 2.7 bitcast_dynamic-update-slice_fusion.4
  180.2 2.6 bitcast_dynamic-update-slice_fusion.3
  182.8 2.7 bitcast_dynamic-update-slice_fusion.2
  185.5 2.6 bitcast_dynamic-update-slice_fusion.1
  188.1 2.6 bitcast_dynamic-update-slice_fusion
  192.7 116.8 %all-reduce.6.cloned.1.call-done = f32[3,512,1024]{1,0,2:T(4,128)} async-done(((f32[3,512,1024]{1,0,2:T(4,128)}), f32[3,512,1024]{1,0,2:T(4,128)}) %all-reduce.6.cloned.1.call-update) | async-done | bytes 6291472
  311.4 54.5 %reduce-scatter.6.cloned.1.call-done = f32[1,8,8,16,512]{4,1,3,2,0:T(8,128)} async-done(((f32[1,8,8,16,1024]{4,1,3,2,0:T(8,128)}), f32[1,8,8,16,512]{4,1,3,2,0:T(8,128)}) %reduce-scatter.6.cloned.1.call-update) | async-done | bytes 2097168 | tf_op jit(solution)/shard_map/reduce_scatter | solution.py:112
  365.9 3.3 fusion.14
  371.0 51.3 %reduce-scatter.4.cloned.1.call-done = f32[1,8,8,16,512]{4,1,3,2,0:T(8,128)} async-done(((f32[1,8,8,16,1024]{4,1,3,2,0:T(8,128)}), f32[1,8,8,16,512]{4,1,3,2,0:T(8,128)}) %reduce-scatter.4.cloned.1.call-update) | async-done | bytes 2097168 | tf_op jit(solution)/shard_map/reduce_scatter | solution.py:103
  422.4 4.3 add_convert_fusion
  429.2 192.7 %reduce-scatter.8.cloned.1.call-done = f32[3,3,64,512]{3,2,1,0:T(8,128)} async-done(((f32[3,3,1024,512]{3,2,1,0:T(8,128)}), f32[3,3,64,512]{3,2,1,0:T(8,128)}) %reduce-scatter.8.cloned.1.call-update) | async-done | bytes 1179664 | tf_op jit(solution)/shard_map/reduce_scatter | solution.py:115
  621.9 2.2 multiply_convert_fusion.1
  (109 shorter events, 33.7 us)
Async XLA Ops:
  7.2 5.4 copy-start
  7.2 43.4 %all-gather.3.cloned.1.call-start = ((), (), s32[]{:S(2)}) async-start(), calls=%async_computation.3 | async-start | bytes 3145728 | tf_op jit(solution)/shard_map/all_gather | solution.py:99
  9.5 5.1 copy-start.9
  9.5 5.2 copy-start.5
  11.8 0.6 copy-start.13
  12.5 3.7 copy-start.11
  14.6 71.2 %all-gather.5.cloned.1.call-start = ((), (), s32[]{:S(2)}) async-start(), calls=%async_computation.5 | async-start | bytes 3145728 | tf_op jit(solution)/shard_map/all_gather | solution.py:107
  16.3 293.2 %all-reduce.6.cloned.1.call-start = ((), (), s32[]{:S(2)}) async-start(), calls=%async_computation.8 | async-start | bytes 16777216
  90.4 1.6 copy-start.3
  92.0 1.9 copy-start.6
  97.7 1.3 copy-start.2
  117.9 4.9 copy-start.4
  139.4 1.2 copy-start.8
  139.4 226.5 %reduce-scatter.6.cloned.1.call-start = ((), (), s32[]{:S(2)}) async-start(), calls=%async_computation.6 | async-start | bytes 6291456 | tf_op jit(solution)/shard_map/reduce_scatter | solution.py:112
  154.5 267.8 %reduce-scatter.4.cloned.1.call-start = ((), (), s32[]{:S(2)}) async-start(), calls=%async_computation.4 | async-start | bytes 6291456 | tf_op jit(solution)/shard_map/reduce_scatter | solution.py:103
  155.4 1.9 copy-start.7
  165.4 1.6 copy-start.15
  165.4 456.4 %reduce-scatter.8.cloned.1.call-start = ((), (), s32[]{:S(2)}) async-start(), calls=%async_computation.7 | async-start | bytes 20054016 | tf_op jit(solution)/shard_map/reduce_scatter | solution.py:115
  190.8 0.7 copy-start.16
  190.8 175.1 %copy-start.1 = (bf16[1,8,8,16,512]{4,3,2,1,0:T(8,128)(2,1)S(1)}, bf16[1,8,8,16,512]{4,3,2,1,0:T(8,128)(2,1)}, u32[]{:S(2)}) copy-start(bf16[1,8,8,16,512]{4,3,2,1,0:T(8,128)(2,1)} %param.4) | copy-start | bytes 3145732
  190.8 175.1 %copy-start.10 = (f32[512]{0:T(512)S(1)}, f32[512]{0:T(512)}, u32[]{:S(2)}) copy-start(f32[512]{0:T(512)} %copy-done.9) | copy-start | bytes 6148
  190.8 175.1 %copy-start.12 = (f32[512]{0:T(512)S(1)}, f32[512]{0:T(512)}, u32[]{:S(2)}) copy-start(f32[512]{0:T(512)} %copy-done.11) | copy-start | bytes 6148
  311.4 58.1 %copy-start.14 = (f32[16]{0:T(128)S(1)}, f32[16]{0:T(128)}, u32[]{:S(2)}) copy-start(f32[16]{0:T(128)} %copy-done.13) | copy-start | bytes 196
Sparse Core Ops, SparseCore 0:
  14.7 35.8 all-gather.2
  52.7 33.1 all-gather.4
  139.5 169.9 all-reduce.5
  311.7 54.1 reduce-scatter.5
  368.0 54.2 reduce-scatter.3
  426.9 194.9 reduce-scatter.7
where the time goes:
time: 639 us; the launch traced here: 631 us
  waiting for transfers between devices  468 us (73%)
  matrix products  62.8 us (10%)
  other arithmetic  45.6 us (7%)
  local copies, waits for them, and re-layouts  39.3 us (6%)
  between operations  15.4 us (2%)
    reduce_scatter x1, waiting for transfers between devices, per_device(): lax.psum_scatter(spatial_local, 'dp', scatter_dimension=2, tiled=True)  193 us
    unnamed x7, waiting for transfers between devices  117 us
    reduce_scatter x1, waiting for transfers between devices, per_device(): lax.psum_scatter(grad_partial, 'tensor', scatter_dimension=4, tiled=True)  54.5 us
    reduce_scatter x1, waiting for transfers between devices, per_device(): lax.psum_scatter(temporal_conv(hidden_second, temporal_weight), 'tensor',...  51.3 us
    all_gather x1, waiting for transfers between devices, per_device(): first_full = lax.all_gather(hidden_first, 'tensor', axis=4, tiled=True)  34.2 us
    conv_general_dilated x2, matrix products, spatial_conv(): lax.conv_general_dilated(flat, kernel, (1, 1), ((1, 1), (1, 1)), dimensio...  27.5 us
    dot_general x9, matrix products, spatial_wgrad(): lax.dot_general(window, right_side, (((0,), (0,)), ((), ())), preferred_e...  23.7 us
    reduce_sum x4, other arithmetic, group_silu(): offsets * lax.rsqrt(spread + 1e-05)  18.3 us
  transfers between devices with their start and end apart: 6, of which 6 were waited for; matrix products, arithmetic and copies ran while one was open for 13% of the time, Pallas kernels for 0%

commit v1 on v0

v1 whole, which is shorter than its diff:
```python
import functools

import jax
import jax.numpy as jnp
from jax import lax
from jax.experimental import pallas as pl
from jax.experimental.pallas import tpu as pltpu
from jax.sharding import PartitionSpec as P

GS = 32
SLOTS = 3
MESH = pl.DeviceIdType.MESH
F32, BF16 = jnp.float32, jnp.bfloat16
NN = (((1,), (0,)), ((), ()))
NT = (((1,), (1,)), ((), ()))
TN = (((0,), (0,)), ((), ()))


def dot(left, right, dims):
    return lax.dot_general(left, right, dims, preferred_element_type=F32)


def bits_reversed(value, size):
    result, step = 0, 1
    while step < size:
        result = result * 2 + (value // step) % 2
        step *= 2
    return result


def kernel(
    T, ND, frames, height, breadth, scale,
    clips, og_in, sw_in, tw_in,
    mixed, cgrad, wgrad,
    sw, tw, first, shifted, gradsp, second, og, acc, gsec, own, ysend, tgot, fgot, same, gbuf, *rest,
):
    stages = ND.bit_length() - 1
    got = rest[:stages]
    load_sem, hf_sem, og_sem, to_sem, gf_sem, rs_send, rs_recv = rest[stages:]
    HW = height * breadth
    POS = frames * HW
    CL = clips.shape[1]
    block = wgrad.shape[1]
    per_slot = CL // block
    me_t = lax.axis_index("tensor")
    me_d = lax.axis_index("dp")
    peers = [lax.rem(me_t + j, T) for j in range(T)]
    owners = [lax.rem(me_t - j + T, T) for j in range(T)]
    bit = [lax.rem(me_d // (1 << s), 2) for s in range(stages)]
    partner = [me_d + (1 - 2 * bit[s]) * (1 << s) for s in range(stages)]

    loads = []
    for j in range(T):
        rows = pl.ds(pl.multiple_of(owners[j] * CL, CL), CL)
        loads.append(pltpu.make_async_copy(sw_in.at[:, rows, :], sw.at[:, j], load_sem.at[0, j]))
        loads.append(pltpu.make_async_copy(tw_in.at[:, :, rows], tw.at[:, j], load_sem.at[1, j]))
    og_load = pltpu.make_async_copy(og_in, og.at[0, pl.ds(HW, POS)], load_sem.at[2, 0])
    og_load.start()
    for load in loads:
        load.start()

    barrier = pltpu.get_barrier_semaphore()
    for j in range(1, T):
        pl.semaphore_signal(barrier, inc=1, device_id={"tensor": peers[j]}, device_id_type=MESH)
    for s in range(stages):
        pl.semaphore_signal(barrier, inc=1, device_id={"dp": partner[s]}, device_id_type=MESH)

    edge = jnp.zeros((frames, breadth, CL), BF16)
    frame = jnp.zeros((HW, CL), BF16)
    for j in range(T):
        first[j, :, :breadth, :] = edge
        first[j, :, breadth + HW :, :] = edge
        og[j, :HW, :] = frame
        og[j, HW + POS :, :] = frame
    gradsp[:, :breadth, :] = edge
    gradsp[:, breadth + HW :, :] = edge
    second[:HW, :] = frame
    second[HW + POS :, :] = frame
    same[...] = jnp.where(
        lax.broadcasted_iota(jnp.int32, (CL, CL), 0) // GS
        == lax.broadcasted_iota(jnp.int32, (CL, CL), 1) // GS,
        1.0,
        0.0,
    ).astype(BF16)

    def group_mean(total):
        high = total.astype(BF16).astype(F32)
        middle = (total - high).astype(BF16).astype(F32)
        low = total - high - middle
        row = lax.broadcasted_iota(jnp.int32, (16, CL), 0)
        terms = jnp.where(row == 0, high, jnp.where(row == 1, middle, jnp.where(row == 2, low, 0.0)))
        summed = dot(terms.astype(BF16), same[...], NN)
        return jnp.sum(summed, axis=0, keepdims=True) * (1.0 / (GS * POS))

    def over_frames(body, count):
        zero = tuple(jnp.zeros((1, CL), F32) for _ in range(count))

        def step(f, sums):
            return tuple(a + jnp.sum(v, axis=0, keepdims=True) for a, v in zip(sums, body(f)))

        return lax.fori_loop(0, frames, step, zero)

    def rows_of(f, offset=0):
        return pl.ds(pl.multiple_of(f * HW + offset, HW), HW)

    def statistics(load):
        center = group_mean(over_frames(lambda f: (load(f),), 1)[0])

        def squares(f):
            offsets = load(f) - center
            return (offsets * offsets,)

        spread = group_mean(over_frames(squares, 1)[0])
        return center, lax.rsqrt(spread + 1e-05)

    def sigmoid(u):
        return 1.0 / (1.0 + jnp.exp(-u))

    def slope(u):
        s = sigmoid(u)
        return s * (1.0 + u * (1.0 - s))

    def pull_back(load, center, rate, grad, put):
        def sums(f):
            unit = (load(f) - center) * rate
            d = grad(f) * slope(unit)
            return d, d * unit

        a, b = over_frames(sums, 2)
        a, b = group_mean(a), group_mean(b)

        def write(f, carry):
            unit = (load(f) - center) * rate
            d = grad(f) * slope(unit)
            put(f, rate * (d - a - unit * b))
            return carry

        lax.fori_loop(0, frames, write, 0)

    def remote(source, target, sends, receives, device):
        return pltpu.make_async_remote_copy(
            src_ref=source, dst_ref=target, send_sem=sends, recv_sem=receives,
            device_id=device, device_id_type=MESH,
        )

    load_clip = lambda f: clips[rows_of(f), :].astype(F32)
    center1, rate1 = statistics(load_clip)
    inside = pl.ds(breadth, HW)

    def put_first(f, carry):
        unit = (load_clip(f) - center1) * rate1
        first[0, f, inside, :] = (unit * sigmoid(unit)).astype(BF16)
        return carry

    lax.fori_loop(0, frames, put_first, 0)
    pl.semaphore_wait(barrier, T - 1 + stages)
    middle = pl.ds(HW, POS)
    hf_copies, og_copies = [], []
    for j in range(1, T):
        hf_copies.append(
            remote(first.at[0, :, inside, :], first.at[j, :, inside, :],
                   hf_sem.at[0, j], hf_sem.at[1, j], {"tensor": peers[j]})
        )
        hf_copies[-1].start()
    og_load.wait()
    for j in range(1, T):
        og_copies.append(
            remote(og.at[0, middle], og.at[j, middle], og_sem.at[0, j], og_sem.at[1, j], {"tensor": peers[j]})
        )
        og_copies[-1].start()
    for load in loads:
        load.wait()

    def shift(load, target, column):
        wide = HW + 2 * breadth
        at = lax.rem(lax.broadcasted_iota(jnp.int32, (wide, CL), 0), breadth)
        keep = at != (0 if column == 0 else breadth - 1)

        def step(f, carry):
            moved = pltpu.roll(load(f).astype(F32), 1 if column == 0 else wide - 1, 0)
            shifted[target, f] = jnp.where(keep, moved, 0.0).astype(BF16)
            return carry

        lax.fori_loop(0, frames, step, 0)

    def window(ref, slot, a):
        rows = pl.ds(pl.multiple_of(a * breadth, breadth), HW)
        return (ref[:, rows, :] if slot is None else ref[slot, :, rows, :]).reshape(POS, CL)

    def conv_slot(j):
        for column in range(3):
            if column == 1:
                ref = first
            else:
                ref = shifted
                shift(lambda f: first[j, f], j, column)

            def tap(a, carry, ref=ref, column=column):
                acc[...] += dot(window(ref, j, a), sw[a * 3 + column, j], NN)
                return carry

            lax.fori_loop(0, 3, tap, 0)

    acc[...] = jnp.zeros_like(acc)
    conv_slot(0)
    for j in range(1, T):
        hf_copies[j - 1].wait_recv()
        conv_slot(j)

    load_out = lambda f: acc[rows_of(f), :]
    center2, rate2 = statistics(load_out)

    def put_second(f, carry):
        unit = (load_out(f) - center2) * rate2
        second[rows_of(f, HW), :] = (unit * sigmoid(unit)).astype(BF16)
        return carry

    lax.fori_loop(0, frames, put_second, 0)

    def temporal(j, target):
        def tap(k, carry):
            target[...] += dot(second[pl.ds(pl.multiple_of(k * HW, HW), POS), :], tw[k, j], NN)
            return carry

        target[...] = jnp.zeros_like(target)
        lax.fori_loop(0, 3, tap, 0)

    to_copies, gf_copies = [], []
    for j in range(1, T):
        temporal(j, own)
        ysend[j - 1] = own[...].astype(BF16)
        to_copies.append(
            remote(ysend.at[j - 1], tgot.at[j - 1], to_sem.at[0, j], to_sem.at[1, j], {"tensor": owners[j]})
        )
        to_copies[-1].start()
    temporal(0, own)

    def back_slot(j):
        def tap(k, carry):
            rows = pl.ds(pl.multiple_of((2 - k) * HW, HW), POS)
            gsec[...] += dot(og[j, rows, :], tw[k, j], NT)
            return carry

        lax.fori_loop(0, 3, tap, 0)

    gsec[...] = jnp.zeros_like(gsec)
    back_slot(0)

    taps = wgrad.shape[0]

    def source(s, n, half):
        size = ND >> (s + 1)
        rows = pl.ds(half * size, size)
        return gbuf.at[lax.rem(n, SLOTS), rows] if s == 0 else got[s - 1].at[n, rows]

    def exchange(s, n):
        return remote(source(s, n, 1 - bit[s]), got[s].at[n], rs_send.at[s, n], rs_recv.at[s, n],
                      {"dp": partner[s]})

    def advance(s, n):
        exchange(s - 1, n).wait_recv()
        total = got[s - 1][n].astype(F32) + source(s - 1, n, bit[s - 1])[...].astype(F32)
        if s < stages:
            got[s - 1][n] = total.astype(BF16)
            exchange(s, n).start()
        else:
            wgrad[n] = (total * scale).reshape(block, CL).astype(BF16)

    def emit(n, slots):
        @pl.when(n >= SLOTS)
        def _():
            exchange(0, n - SLOTS).wait_send()

        for j in range(T):
            place = bits_reversed(owners[j], T)
            product = slots(j)
            for b in range(per_slot):
                gbuf[lax.rem(n, SLOTS), bits_reversed(b, per_slot) * T + place] = (
                    product[b * block : (b + 1) * block].astype(BF16)
                )
        exchange(0, n).start()

        @pl.when(n >= 1)
        def _():
            advance(1, n - 1)

    for j in range(1, T):
        og_copies[j - 1].wait_recv()

    def temporal_tap(k, carry):
        rows = pl.ds(pl.multiple_of(k * HW, HW), POS)
        emit(k, lambda j: dot(og[j, middle, :], second[rows, :], TN))
        return carry

    lax.fori_loop(0, 3, temporal_tap, 0)

    for j in range(1, T):
        back_slot(j)

    def put_gradsp(f, value):
        gradsp[f, inside, :] = value.astype(BF16)

    pull_back(load_out, center2, rate2, lambda f: gsec[rows_of(f), :], put_gradsp)

    done = {s: 0 for s in range(2, stages + 1)}

    def move(s, upto):
        for n in range(done[s], min(upto, taps)):
            advance(s, n)
        done[s] = max(done[s], min(upto, taps))

    for column in range(3):
        if column == 1:
            ref = first
        else:
            ref = shifted
            for j in range(T):
                shift(lambda f, j=j: first[j, f], j, column)

        def spatial_tap(a, carry, ref=ref, column=column):
            emit(3 + column * 3 + a, lambda j: dot(window(ref, j, a), window(gradsp, None, 1), TN))
            return carry

        lax.fori_loop(0, 3, spatial_tap, 0)
        for s in range(2, stages + 1):
            move(s, 2 * column + 2 - 2 * (s - 2))
    advance(1, taps - 1)

    def grad_slot(j):
        acc[...] = jnp.zeros_like(acc)
        for column in range(3):
            if column == 1:
                ref, slot = gradsp, None
            else:
                ref, slot = shifted, 0
                shift(lambda f: gradsp[f], 0, column)

            def tap(a, carry, ref=ref, slot=slot, column=column):
                acc[...] += dot(window(ref, slot, a), sw[(2 - a) * 3 + 2 - column, j], NT)
                return carry

            lax.fori_loop(0, 3, tap, 0)

    for j in range(1, T):
        grad_slot(j)
        to_copies[j - 1].wait_send()
        ysend[j - 1] = acc[...].astype(BF16)
        gf_copies.append(
            remote(ysend.at[j - 1], fgot.at[j - 1], gf_sem.at[0, j], gf_sem.at[1, j], {"tensor": owners[j]})
        )
        gf_copies[-1].start()
    for s in range(2, stages + 1):
        move(s, 7 - (s - 2))
    grad_slot(0)
    for s in range(2, stages + 1):
        move(s, 8 - (s - 2))

    for j in range(1, T):
        to_copies[j - 1].wait_recv()

    def put_mixed(f, carry):
        rows = rows_of(f)
        total = load_clip(f) + own[rows, :]
        for j in range(1, T):
            total = total + tgot[j - 1, rows, :].astype(F32)
        mixed[rows, :] = total.astype(BF16)
        return carry

    lax.fori_loop(0, frames, put_mixed, 0)
    for s in range(2, stages + 1):
        move(s, 10 - (s - 2))

    for j in range(1, T):
        gf_copies[j - 1].wait_recv()

    def grad_first(f):
        total = acc[rows_of(f), :]
        for j in range(1, T):
            total = total + fgot[j - 1, rows_of(f), :].astype(F32)
        return total

    def put_clip(f, value):
        cgrad[rows_of(f), :] = (og[0, rows_of(f, HW), :].astype(F32) + value).astype(BF16)

    pull_back(load_clip, center1, rate1, grad_first, put_clip)

    for n in range(10, taps + stages):
        for s in range(2, stages + 1):
            move(s, n + 1 - (s - 2))

    for copy in hf_copies + og_copies + gf_copies:
        copy.wait_send()
    for n in range(max(0, taps - SLOTS), taps):
        exchange(0, n).wait_send()

    def drain(n, carry):
        for s in range(1, stages):
            exchange(s, n).wait_send()
        return carry

    lax.fori_loop(0, taps, drain, 0)


def per_device(clips, out_grad, spatial_weight, temporal_weight):
    T, ND = lax.axis_size("tensor"), lax.axis_size("dp")
    _, frames, height, breadth, CL = clips.shape
    HW = height * breadth
    POS = frames * HW
    block = spatial_weight.shape[2] // ND
    stages = ND.bit_length() - 1
    taps = 12
    scale = 1.0 / float(POS * ND) ** 0.5
    hbm = pl.BlockSpec(memory_space=pl.ANY)
    vmem = pl.BlockSpec(memory_space=pltpu.VMEM)
    dma = pltpu.SemaphoreType.DMA
    wide = HW + 2 * breadth
    scratch = [
        pltpu.VMEM((9, T, CL, CL), BF16),
        pltpu.VMEM((3, T, CL, CL), BF16),
        pltpu.VMEM((T, frames, wide, CL), BF16),
        pltpu.VMEM((T, frames, wide, CL), BF16),
        pltpu.VMEM((frames, wide, CL), BF16),
        pltpu.VMEM((POS + 2 * HW, CL), BF16),
        pltpu.VMEM((T, POS + 2 * HW, CL), BF16),
        pltpu.VMEM((POS, CL), F32),
        pltpu.VMEM((POS, CL), F32),
        pltpu.VMEM((POS, CL), F32),
        pltpu.VMEM((T - 1, POS, CL), BF16),
        pltpu.VMEM((T - 1, POS, CL), BF16),
        pltpu.VMEM((T - 1, POS, CL), BF16),
        pltpu.VMEM((CL, CL), BF16),
        pltpu.VMEM((SLOTS, ND, block, CL), BF16),
    ]
    scratch += [pltpu.VMEM((taps, ND >> (s + 1), block, CL), BF16) for s in range(stages)]
    scratch += [dma((3, T)), dma((2, T)), dma((2, T)), dma((2, T)), dma((2, T))]
    scratch += [dma((stages, taps)), dma((stages, taps))]
    mixed, clip_grad, grads = pl.pallas_call(
        functools.partial(kernel, T, ND, frames, height, breadth, scale),
        out_shape=(
            jax.ShapeDtypeStruct((POS, CL), BF16),
            jax.ShapeDtypeStruct((POS, CL), BF16),
            jax.ShapeDtypeStruct((taps, block, CL), BF16),
        ),
        in_specs=[vmem, hbm, hbm, hbm],
        out_specs=(vmem, vmem, vmem),
        scratch_shapes=scratch,
        compiler_params=pltpu.CompilerParams(
            collective_id=0, has_side_effects=True, vmem_limit_bytes=63 * 1024 * 1024
        ),
        cost_estimate=pl.CostEstimate(
            flops=24 * POS * 3 * T * CL * CL, bytes_accessed=20 * 2**20, transcendentals=4 * POS * CL
        ),
    )(
        clips.reshape(POS, CL),
        out_grad.reshape(POS, CL),
        spatial_weight.reshape(9, T * CL, CL),
        temporal_weight,
    )
    spatial = jnp.transpose(grads[3:].reshape(3, 3, block, CL), (1, 0, 2, 3))
    return (
        mixed.reshape(clips.shape),
        clip_grad.reshape(clips.shape),
        spatial,
        jnp.transpose(grads[:3], (0, 2, 1)),
    )


def solution(mesh):
    placed = (
        P("dp", None, None, None, "tensor"),
        P("dp", None, None, None, "tensor"),
        P(None, None, None, "tensor"),
        P(None, "tensor", None),
    )
    return jax.shard_map(
        per_device,
        mesh=mesh,
        in_specs=placed,
        out_specs=(
            P("dp", None, None, None, "tensor"),
            P("dp", None, None, None, "tensor"),
            P(None, None, "dp", "tensor"),
            P(None, "tensor", "dp"),
        ),
        check_vma=False,
    )
```

time: 639 us -> 155 us (0.24); the launches traced: 631 us -> 155 us
  waiting for transfers between devices: 468 us -> 0 us
  Pallas kernels: 0 us -> 146 us
  matrix products: 62.8 us -> 0 us
  other arithmetic: 45.6 us -> 0 us
  local copies, waits for them, and re-layouts: 39.3 us -> 8.1 us
  between operations: 15.4 us -> 0.64 us
    reduce_scatter x3 -> x0, waiting for transfers between devices: 299 us -> none  [the longest x1 193 us: per_device(): lax.psum_scatter(spatial_local, 'dp', scatter_dimension=2, tiled=True)]
    pallas_call x0 -> x1, Pallas kernels: none -> 146 us  [per_device(): pl.pallas_call(functools.partial(kernel, T, ND, frames, height, breadth,...]
    unnamed x7 -> x0, waiting for transfers between devices: 117 us -> none
    all_gather x2 -> x0, waiting for transfers between devices: 52.3 us -> none  [the longest x1 34.2 us: per_device(): first_full = lax.all_gather(hidden_first, 'tensor', axis=4, tiled=True)]
    dot_general x18 -> x0, matrix products: 35.2 us -> none  [the longest x9 23.7 us: spatial_wgrad(): lax.dot_general(window, right_side, (((0,), (0,)), ((), ())), preferred_e...]
    reduce_sum x15 -> x0, other arithmetic: 27.8 us -> none  [the longest x4 18.3 us: group_silu(): offsets * lax.rsqrt(spread + 1e-05)]
    conv_general_dilated x2 -> x0, matrix products: 27.5 us -> none  [spatial_conv(): lax.conv_general_dilated(flat, kernel, (1, 1), ((1, 1), (1, 1)), dimensio...]
    convert_element_type x5 -> x0, other arithmetic: 14.6 us -> none  [the longest x1 4.88 us: per_device(): grad_spatial = pull_second(grad_second)[0].astype(jnp.bfloat16)]
  transfers between devices with their start and end apart: 6 -> 0, of which waited for: 6 -> 0; matrix products, arithmetic and copies ran while one was open for 13% -> 0% of each run, Pallas kernels for 0% -> 0%
where the time goes in v1:
time: 155 us
  Pallas kernels  146 us (94%)
  local copies, waits for them, and re-layouts  8.1 us (5%)
    pallas_call x1, Pallas kernels, per_device(): pl.pallas_call(functools.partial(kernel, T, ND, frames, height, breadth,...  146 us
    unnamed x2, local copies, waits for them, and re-layouts  4.52 us

profile of v1, /device:TPU:0, one launch (start us, length us, event | category | flops | bytes accessed | tf_op | source)
XLA Modules:
  0.0 154.6 jit_solution(5764451060967993488)
XLA Ops:
  0.6 145.9 %shard_map.75 = (bf16[1024,512]{1,0:T(8,128)(2,1)}, bf16[1024,512]{1,0:T(8,128)(2,1)}, bf16[12,64,512]{2,1,0:T(8,128)(2,1)}) custom-call(bf16[1024,512]{1,0:T(8,128)(2,1)} %bitcast.16, bf16[1024,512]{1,0:T(8,128)(2,1)} %bitcast.17, bf16[9,1024,512]{2,1,0:T(8,128)(2,1)} %bitcast.15, bf16[3,512,1024]{2,1,0:T(8,128)(2,1)} %tw_in.1), custom_call_target="tpu_custom_call" | custom-call | flops 38654705664 | bytes 20971520 | tf_op jit(solution)/shard_map/pallas_call | solution.py:437
  146.5 1.6 %slice_bitcast_fusion = bf16[3,512,64]{1,2,0:T(8,128)(2,1)} fusion(bf16[12,64,512]{2,1,0:T(8,128)(2,1)} %get-tuple-element.9), kind=kLoop, calls=%fused_computation.1 | loop fusion | bytes 393216 | tf_op jit(solution)/shard_map/transpose | solution.py:464
  148.1 1.1 slice.6
  149.2 0.9 copy.10
  150.1 2.3 %copy.13 = bf16[1,8,8,16,512]{4,3,2,1,0:T(8,128)(2,1)} copy(bf16[1,8,8,16,512]{4,3,2,1,0:T(8,128)(2,1)} %bitcast.13) | data formatting | bytes 2097152
  152.3 2.3 %copy.14 = bf16[1,8,8,16,512]{4,3,2,1,0:T(8,128)(2,1)} copy(bf16[1,8,8,16,512]{4,3,2,1,0:T(8,128)(2,1)} %bitcast.12) | data formatting | bytes 2097152

commit v2 on v1

--- a/solution.py
+++ b/solution.py
@@ -31,8 +31,8 @@
 def kernel(
     T, ND, frames, height, breadth, scale,
     clips, og_in, sw_in, tw_in,
-    mixed, cgrad, wgrad,
-    sw, tw, first, shifted, gradsp, second, og, acc, gsec, own, ysend, tgot, fgot, same, gbuf, *rest,
+    mixed, cgrad, wgrad, tgrad,
+    sw, tw, first, shifted, gradsp, second, og, acc, gsec, own, ysend, fsend, tgot, fgot, same, gbuf, *rest,
 ):
     stages = ND.bit_length() - 1
     got = rest[:stages]
@@ -41,6 +41,7 @@
     POS = frames * HW
     CL = clips.shape[1]
     block = wgrad.shape[1]
+    early, half = frames // 4, frames // 2
     per_slot = CL // block
     me_t = lax.axis_index("tensor")
     me_d = lax.axis_index("dp")
@@ -143,6 +144,18 @@
             device_id=device, device_id_type=MESH,
         )
 
+    middle = pl.ds(HW, POS)
+    og_copies = []
+    for j, part in [(j, part) for part in range(2) for j in range(1, T)]:
+        some = pl.ds(HW * (1 + early * part), HW * (frames - early if part else early))
+        og_copies.append(
+            remote(og.at[0, some], og.at[j, some], og_sem.at[part, j], og_sem.at[2 + part, j], {"tensor": peers[j]})
+        )
+    og_load.wait()
+    pl.semaphore_wait(barrier, T - 1 + stages)
+    for copy in og_copies[: T - 1]:
+        copy.start()
+
     load_clip = lambda f: clips[rows_of(f), :].astype(F32)
     center1, rate1 = statistics(load_clip)
     inside = pl.ds(breadth, HW)
@@ -153,25 +166,20 @@
         return carry
 
     lax.fori_loop(0, frames, put_first, 0)
-    pl.semaphore_wait(barrier, T - 1 + stages)
-    middle = pl.ds(HW, POS)
-    hf_copies, og_copies = [], []
-    for j in range(1, T):
+    hf_copies = []
+    for j, part in [(j, part) for part in range(2) for j in range(1, T)]:
+        some = pl.ds(part * half, frames - half if part else half)
         hf_copies.append(
-            remote(first.at[0, :, inside, :], first.at[j, :, inside, :],
-                   hf_sem.at[0, j], hf_sem.at[1, j], {"tensor": peers[j]})
+            remote(first.at[0, some, inside, :], first.at[j, some, inside, :],
+                   hf_sem.at[part, j], hf_sem.at[2 + part, j], {"tensor": peers[j]})
         )
         hf_copies[-1].start()
-    og_load.wait()
-    for j in range(1, T):
-        og_copies.append(
-            remote(og.at[0, middle], og.at[j, middle], og_sem.at[0, j], og_sem.at[1, j], {"tensor": peers[j]})
-        )
-        og_copies[-1].start()
+    for copy in og_copies[T - 1 :]:
+        copy.start()
     for load in loads:
         load.wait()
 
-    def shift(load, target, column):
+    def shift(load, target, column, begin=0, end=frames):
         wide = HW + 2 * breadth
         at = lax.rem(lax.broadcasted_iota(jnp.int32, (wide, CL), 0), breadth)
         keep = at != (0 if column == 0 else breadth - 1)
@@ -181,31 +189,35 @@
             shifted[target, f] = jnp.where(keep, moved, 0.0).astype(BF16)
             return carry
 
-        lax.fori_loop(0, frames, step, 0)
-
-    def window(ref, slot, a):
+        lax.fori_loop(begin, end, step, 0)
+
+    def window(ref, slot, a, begin=0, end=frames):
         rows = pl.ds(pl.multiple_of(a * breadth, breadth), HW)
-        return (ref[:, rows, :] if slot is None else ref[slot, :, rows, :]).reshape(POS, CL)
-
-    def conv_slot(j):
+        if slot is None:
+            return ref[begin:end, rows, :].reshape((end - begin) * HW, CL)
+        return ref[slot, begin:end, rows, :].reshape((end - begin) * HW, CL)
+
+    def conv_slot(j, begin=0, end=frames):
+        out = pl.ds(begin * HW, (end - begin) * HW)
         for column in range(3):
             if column == 1:
                 ref = first
             else:
                 ref = shifted
-                shift(lambda f: first[j, f], j, column)
+                shift(lambda f: first[j, f], j, column, begin, end)
 
             def tap(a, carry, ref=ref, column=column):
-                acc[...] += dot(window(ref, j, a), sw[a * 3 + column, j], NN)
+                acc[out, :] += dot(window(ref, j, a, begin, end), sw[a * 3 + column, j], NN)
                 return carry
 
             lax.fori_loop(0, 3, tap, 0)
 
     acc[...] = jnp.zeros_like(acc)
     conv_slot(0)
-    for j in range(1, T):
-        hf_copies[j - 1].wait_recv()
-        conv_slot(j)
+    for part in range(2):
+        for j in range(1, T):
+            hf_copies[part * (T - 1) + j - 1].wait_recv()
+            conv_slot(j, part * half, frames if part else half)
 
     load_out = lambda f: acc[rows_of(f), :]
     center2, rate2 = statistics(load_out)
@@ -233,7 +245,6 @@
             remote(ysend.at[j - 1], tgot.at[j - 1], to_sem.at[0, j], to_sem.at[1, j], {"tensor": owners[j]})
         )
         to_copies[-1].start()
-    temporal(0, own)
 
     def back_slot(j):
         def tap(k, carry):
@@ -243,10 +254,8 @@
 
         lax.fori_loop(0, 3, tap, 0)
 
-    gsec[...] = jnp.zeros_like(gsec)
-    back_slot(0)
-
-    taps = wgrad.shape[0]
+    taps = wgrad.shape[0] + tgrad.shape[0]
+    columns = (1, 0, 2)
 
     def source(s, n, half):
         size = ND >> (s + 1)
@@ -264,7 +273,11 @@
             got[s - 1][n] = total.astype(BF16)
             exchange(s, n).start()
         else:
-            wgrad[n] = (total * scale).reshape(block, CL).astype(BF16)
+            value = (total * scale).reshape(block, CL).astype(BF16)
+            if n < 3:
+                tgrad[n] = value
+            else:
+                wgrad[(n - 3) % 3 * 3 + columns[(n - 3) // 3]] = value
 
     def emit(n, slots):
         @pl.when(n >= SLOTS)
@@ -284,8 +297,8 @@
         def _():
             advance(1, n - 1)
 
-    for j in range(1, T):
-        og_copies[j - 1].wait_recv()
+    for copy in og_copies:
+        copy.wait_recv()
 
     def temporal_tap(k, carry):
         rows = pl.ds(pl.multiple_of(k * HW, HW), POS)
@@ -294,7 +307,8 @@
 
     lax.fori_loop(0, 3, temporal_tap, 0)
 
-    for j in range(1, T):
+    gsec[...] = jnp.zeros_like(gsec)
+    for j in range(T):
         back_slot(j)
 
     def put_gradsp(f, value):
@@ -309,7 +323,12 @@
             advance(s, n)
         done[s] = max(done[s], min(upto, taps))
 
-    for column in range(3):
+    def pace(upto):
+        for s in range(2, stages + 1):
+            move(s, upto - (s - 2))
+
+    def spatial_taps(place):
+        column = columns[place]
         if column == 1:
             ref = first
         else:
@@ -317,14 +336,11 @@
             for j in range(T):
                 shift(lambda f, j=j: first[j, f], j, column)
 
-        def spatial_tap(a, carry, ref=ref, column=column):
-            emit(3 + column * 3 + a, lambda j: dot(window(ref, j, a), window(gradsp, None, 1), TN))
+        def tap(a, carry):
+            emit(3 + place * 3 + a, lambda j: dot(window(ref, j, a), window(gradsp, None, 1), TN))
             return carry
 
-        lax.fori_loop(0, 3, spatial_tap, 0)
-        for s in range(2, stages + 1):
-            move(s, 2 * column + 2 - 2 * (s - 2))
-    advance(1, taps - 1)
+        lax.fori_loop(0, 3, tap, 0)
 
     def grad_slot(j):
         acc[...] = jnp.zeros_like(acc)
@@ -341,19 +357,24 @@
 
             lax.fori_loop(0, 3, tap, 0)
 
+    spatial_taps(0)
+    pace(3)
     for j in range(1, T):
         grad_slot(j)
-        to_copies[j - 1].wait_send()
-        ysend[j - 1] = acc[...].astype(BF16)
+        fsend[j - 1] = acc[...].astype(BF16)
         gf_copies.append(
-            remote(ysend.at[j - 1], fgot.at[j - 1], gf_sem.at[0, j], gf_sem.at[1, j], {"tensor": owners[j]})
+            remote(fsend.at[j - 1], fgot.at[j - 1], gf_sem.at[0, j], gf_sem.at[1, j], {"tensor": owners[j]})
         )
         gf_copies[-1].start()
-    for s in range(2, stages + 1):
-        move(s, 7 - (s - 2))
+    pace(4)
+    spatial_taps(1)
+    pace(6)
+    spatial_taps(2)
+    advance(1, taps - 1)
+    pace(7)
     grad_slot(0)
-    for s in range(2, stages + 1):
-        move(s, 8 - (s - 2))
+    pace(9)
+    temporal(0, own)
 
     for j in range(1, T):
         to_copies[j - 1].wait_recv()
@@ -367,8 +388,7 @@
         return carry
 
     lax.fori_loop(0, frames, put_mixed, 0)
-    for s in range(2, stages + 1):
-        move(s, 10 - (s - 2))
+    pace(10)
 
     for j in range(1, T):
         gf_copies[j - 1].wait_recv()
@@ -385,10 +405,9 @@
     pull_back(load_clip, center1, rate1, grad_first, put_clip)
 
     for n in range(10, taps + stages):
-        for s in range(2, stages + 1):
-            move(s, n + 1 - (s - 2))
-
-    for copy in hf_copies + og_copies + gf_copies:
+        pace(n + 1)
+
+    for copy in hf_copies + og_copies + to_copies + gf_copies:
         copy.wait_send()
     for n in range(max(0, taps - SLOTS), taps):
         exchange(0, n).wait_send()
@@ -428,21 +447,23 @@
         pltpu.VMEM((T - 1, POS, CL), BF16),
         pltpu.VMEM((T - 1, POS, CL), BF16),
         pltpu.VMEM((T - 1, POS, CL), BF16),
+        pltpu.VMEM((T - 1, POS, CL), BF16),
         pltpu.VMEM((CL, CL), BF16),
         pltpu.VMEM((SLOTS, ND, block, CL), BF16),
     ]
     scratch += [pltpu.VMEM((taps, ND >> (s + 1), block, CL), BF16) for s in range(stages)]
-    scratch += [dma((3, T)), dma((2, T)), dma((2, T)), dma((2, T)), dma((2, T))]
+    scratch += [dma((3, T)), dma((4, T)), dma((4, T)), dma((2, T)), dma((2, T))]
     scratch += [dma((stages, taps)), dma((stages, taps))]
-    mixed, clip_grad, grads = pl.pallas_call(
+    mixed, clip_grad, spatial, temporal = pl.pallas_call(
         functools.partial(kernel, T, ND, frames, height, breadth, scale),
         out_shape=(
             jax.ShapeDtypeStruct((POS, CL), BF16),
             jax.ShapeDtypeStruct((POS, CL), BF16),
-            jax.ShapeDtypeStruct((taps, block, CL), BF16),
+            jax.ShapeDtypeStruct((taps - 3, block, CL), BF16),
+            jax.ShapeDtypeStruct((3, block, CL), BF16),
         ),
         in_specs=[vmem, hbm, hbm, hbm],
-        out_specs=(vmem, vmem, vmem),
+        out_specs=(vmem, vmem, vmem, vmem),
         scratch_shapes=scratch,
         compiler_params=pltpu.CompilerParams(
             collective_id=0, has_side_effects=True, vmem_limit_bytes=63 * 1024 * 1024
@@ -456,12 +477,11 @@
         spatial_weight.reshape(9, T * CL, CL),
         temporal_weight,
     )
-    spatial = jnp.transpose(grads[3:].reshape(3, 3, block, CL), (1, 0, 2, 3))
     return (
         mixed.reshape(clips.shape),
         clip_grad.reshape(clips.shape),
-        spatial,
-        jnp.transpose(grads[:3], (0, 2, 1)),
+        spatial.reshape(3, 3, block, CL),
+        jnp.transpose(temporal, (0, 2, 1)),
     )
 
 

time: 155 us -> 162 us (1.045)
  Pallas kernels: 146 us -> 153 us
    pallas_call x1, Pallas kernels: 146 us -> 153 us  [per_device(): pl.pallas_call(functools.partial(kernel, T, ND, frames, height, breadth,...]
    unnamed x2 -> x4, local copies, waits for them, and re-layouts: 4.52 us -> 8.06 us
where the time goes in v2:
time: 162 us
  Pallas kernels  153 us (94%)
  local copies, waits for them, and re-layouts  8.06 us (5%)
    pallas_call x1, Pallas kernels, per_device(): pl.pallas_call(functools.partial(kernel, T, ND, frames, height, breadth,...  153 us
    unnamed x4, local copies, waits for them, and re-layouts  8.06 us

profile of v2, /device:TPU:0, one launch (start us, length us, event | category | flops | bytes accessed | tf_op | source)
XLA Modules:
  0.0 161.6 jit_solution(14975668867140683803)
XLA Ops:
  0.6 152.9 %shard_map.75 = (bf16[1024,512]{1,0:T(8,128)(2,1)}, bf16[1024,512]{1,0:T(8,128)(2,1)}, bf16[9,64,512]{2,1,0:T(8,128)(2,1)}, bf16[3,64,512]{2,1,0:T(8,128)(2,1)}) custom-call(bf16[1024,512]{1,0:T(8,128)(2,1)} %bitcast.12, bf16[1024,512]{1,0:T(8,128)(2,1)} %bitcast.13, bf16[9,1024,512]{2,1,0:T(8,128)(2,1)} %bitcast.11, bf16[3,512,1024]{2,1,0:T(8,128)(2,1)} %tw_in.1), custom_call_target="tpu_custom_call" | custom-call | flops 38654705664 | bytes 20971520 | tf_op jit(solution)/shard_map/pallas_call | solution.py:457
  153.5 2.3 %copy.12 = bf16[1,8,8,16,512]{4,3,2,1,0:T(8,128)(2,1)} copy(bf16[1,8,8,16,512]{4,3,2,1,0:T(8,128)(2,1)} %bitcast.8) | data formatting | bytes 2097152
  155.8 2.3 %copy.13 = bf16[1,8,8,16,512]{4,3,2,1,0:T(8,128)(2,1)} copy(bf16[1,8,8,16,512]{4,3,2,1,0:T(8,128)(2,1)} %bitcast.7) | data formatting | bytes 2097152
  158.0 1.9 %copy.14 = bf16[3,3,64,512]{3,2,1,0:T(8,128)(2,1)} copy(bf16[3,3,64,512]{3,2,1,0:T(8,128)(2,1)} %bitcast.9) | data formatting | bytes 1179648
  160.0 1.6 copy.15

commit v3 on v2

--- a/solution.py
+++ b/solution.py
@@ -13,7 +13,6 @@
 F32, BF16 = jnp.float32, jnp.bfloat16
 NN = (((1,), (0,)), ((), ()))
 NT = (((1,), (1,)), ((), ()))
-TN = (((0,), (0,)), ((), ()))
 
 
 def dot(left, right, dims):
@@ -32,7 +31,7 @@
     T, ND, frames, height, breadth, scale,
     clips, og_in, sw_in, tw_in,
     mixed, cgrad, wgrad, tgrad,
-    sw, tw, first, shifted, gradsp, second, og, acc, gsec, own, ysend, fsend, tgot, fgot, same, gbuf, *rest,
+    sw, tw, first, shifted, gradsp, second, og, first_t, og_t, acc, gsec, own, ysend, fsend, tgot, fgot, same, gbuf, *rest,
 ):
     stages = ND.bit_length() - 1
     got = rest[:stages]
@@ -41,7 +40,7 @@
     POS = frames * HW
     CL = clips.shape[1]
     block = wgrad.shape[1]
-    early, half = frames // 4, frames // 2
+    half = frames // 2
     per_slot = CL // block
     me_t = lax.axis_index("tensor")
     me_d = lax.axis_index("dp")
@@ -146,15 +145,11 @@
 
     middle = pl.ds(HW, POS)
     og_copies = []
-    for j, part in [(j, part) for part in range(2) for j in range(1, T)]:
-        some = pl.ds(HW * (1 + early * part), HW * (frames - early if part else early))
+    for j in range(1, T):
         og_copies.append(
-            remote(og.at[0, some], og.at[j, some], og_sem.at[part, j], og_sem.at[2 + part, j], {"tensor": peers[j]})
+            remote(og.at[0, middle], og.at[j, middle], og_sem.at[0, j], og_sem.at[1, j], {"tensor": peers[j]})
         )
     og_load.wait()
-    pl.semaphore_wait(barrier, T - 1 + stages)
-    for copy in og_copies[: T - 1]:
-        copy.start()
 
     load_clip = lambda f: clips[rows_of(f), :].astype(F32)
     center1, rate1 = statistics(load_clip)
@@ -166,6 +161,7 @@
         return carry
 
     lax.fori_loop(0, frames, put_first, 0)
+    pl.semaphore_wait(barrier, T - 1 + stages)
     hf_copies = []
     for j, part in [(j, part) for part in range(2) for j in range(1, T)]:
         some = pl.ds(part * half, frames - half if part else half)
@@ -174,7 +170,7 @@
                    hf_sem.at[part, j], hf_sem.at[2 + part, j], {"tensor": peers[j]})
         )
         hf_copies[-1].start()
-    for copy in og_copies[T - 1 :]:
+    for copy in og_copies:
         copy.start()
     for load in loads:
         load.wait()
@@ -197,23 +193,38 @@
             return ref[begin:end, rows, :].reshape((end - begin) * HW, CL)
         return ref[slot, begin:end, rows, :].reshape((end - begin) * HW, CL)
 
+    def turn(load, target, j, begin=0, end=frames):
+        def step(f, carry):
+            target[j, :, rows_of(f)] = jnp.transpose(load(f))
+            return carry
+
+        lax.fori_loop(begin, end, step, 0)
+
+    def turn_first(j, begin=0, end=frames):
+        turn(lambda f: first[j, f, inside, :], first_t, j, begin, end)
+
+    def turn_og(j):
+        turn(lambda f: og[j, rows_of(f, HW), :], og_t, j)
+
     def conv_slot(j, begin=0, end=frames):
         out = pl.ds(begin * HW, (end - begin) * HW)
         for column in range(3):
             if column == 1:
-                ref = first
+                ref, slot = first, j
             else:
-                ref = shifted
-                shift(lambda f: first[j, f], j, column, begin, end)
-
-            def tap(a, carry, ref=ref, column=column):
-                acc[out, :] += dot(window(ref, j, a, begin, end), sw[a * 3 + column, j], NN)
+                ref, slot = shifted, 0
+                shift(lambda f: first[j, f], 0, column, begin, end)
+
+            def tap(a, carry, ref=ref, slot=slot, column=column):
+                acc[out, :] += dot(window(ref, slot, a, begin, end), sw[a * 3 + column, j], NN)
                 return carry
 
             lax.fori_loop(0, 3, tap, 0)
 
     acc[...] = jnp.zeros_like(acc)
     conv_slot(0)
+    turn_first(0)
+    turn_og(0)
     for part in range(2):
         for j in range(1, T):
             hf_copies[part * (T - 1) + j - 1].wait_recv()
@@ -245,6 +256,9 @@
             remote(ysend.at[j - 1], tgot.at[j - 1], to_sem.at[0, j], to_sem.at[1, j], {"tensor": owners[j]})
         )
         to_copies[-1].start()
+
+    for j in range(1, T):
+        turn_first(j)
 
     def back_slot(j):
         def tap(k, carry):
@@ -297,18 +311,20 @@
         def _():
             advance(1, n - 1)
 
-    for copy in og_copies:
-        copy.wait_recv()
+    gsec[...] = jnp.zeros_like(gsec)
+    back_slot(0)
+    for j in range(1, T):
+        og_copies[j - 1].wait_recv()
+        turn_og(j)
 
     def temporal_tap(k, carry):
         rows = pl.ds(pl.multiple_of(k * HW, HW), POS)
-        emit(k, lambda j: dot(og[j, middle, :], second[rows, :], TN))
+        emit(k, lambda j: dot(og_t[j], second[rows, :], NN))
         return carry
 
     lax.fori_loop(0, 3, temporal_tap, 0)
 
-    gsec[...] = jnp.zeros_like(gsec)
-    for j in range(T):
+    for j in range(1, T):
         back_slot(j)
 
     def put_gradsp(f, value):
@@ -328,16 +344,14 @@
             move(s, upto - (s - 2))
 
     def spatial_taps(place):
-        column = columns[place]
-        if column == 1:
-            ref = first
+        if columns[place] == 1:
+            ref, slot = gradsp, None
         else:
-            ref = shifted
-            for j in range(T):
-                shift(lambda f, j=j: first[j, f], j, column)
+            ref, slot = shifted, 0
+            shift(lambda f: gradsp[f], 0, 2 - columns[place])
 
         def tap(a, carry):
-            emit(3 + place * 3 + a, lambda j: dot(window(ref, j, a), window(gradsp, None, 1), TN))
+            emit(3 + place * 3 + a, lambda j: dot(first_t[j], window(ref, slot, 2 - a), NN))
             return carry
 
         lax.fori_loop(0, 3, tap, 0)
@@ -358,7 +372,12 @@
             lax.fori_loop(0, 3, tap, 0)
 
     spatial_taps(0)
-    pace(3)
+    pace(2)
+    spatial_taps(1)
+    pace(4)
+    spatial_taps(2)
+    advance(1, taps - 1)
+    pace(5)
     for j in range(1, T):
         grad_slot(j)
         fsend[j - 1] = acc[...].astype(BF16)
@@ -366,14 +385,9 @@
             remote(fsend.at[j - 1], fgot.at[j - 1], gf_sem.at[0, j], gf_sem.at[1, j], {"tensor": owners[j]})
         )
         gf_copies[-1].start()
-    pace(4)
-    spatial_taps(1)
-    pace(6)
-    spatial_taps(2)
-    advance(1, taps - 1)
     pace(7)
     grad_slot(0)
-    pace(9)
+    pace(8)
     temporal(0, own)
 
     for j in range(1, T):
@@ -437,10 +451,12 @@
         pltpu.VMEM((9, T, CL, CL), BF16),
         pltpu.VMEM((3, T, CL, CL), BF16),
         pltpu.VMEM((T, frames, wide, CL), BF16),
-        pltpu.VMEM((T, frames, wide, CL), BF16),
+        pltpu.VMEM((1, frames, wide, CL), BF16),
         pltpu.VMEM((frames, wide, CL), BF16),
         pltpu.VMEM((POS + 2 * HW, CL), BF16),
         pltpu.VMEM((T, POS + 2 * HW, CL), BF16),
+        pltpu.VMEM((T, CL, POS), BF16),
+        pltpu.VMEM((T, CL, POS), BF16),
         pltpu.VMEM((POS, CL), F32),
         pltpu.VMEM((POS, CL), F32),
         pltpu.VMEM((POS, CL), F32),
@@ -452,7 +468,7 @@
         pltpu.VMEM((SLOTS, ND, block, CL), BF16),
     ]
     scratch += [pltpu.VMEM((taps, ND >> (s + 1), block, CL), BF16) for s in range(stages)]
-    scratch += [dma((3, T)), dma((4, T)), dma((4, T)), dma((2, T)), dma((2, T))]
+    scratch += [dma((3, T)), dma((4, T)), dma((2, T)), dma((2, T)), dma((2, T))]
     scratch += [dma((stages, taps)), dma((stages, taps))]
     mixed, clip_grad, spatial, temporal = pl.pallas_call(
         functools.partial(kernel, T, ND, frames, height, breadth, scale),

time: 162 us -> 160 us (0.988); the launches traced: 162 us -> 157 us
  Pallas kernels: 153 us -> 148 us
    pallas_call x1, Pallas kernels: 153 us -> 148 us  [per_device(): pl.pallas_call(functools.partial(kernel, T, ND, frames, height, breadth,...]
where the time goes in v3:
time: 160 us; the launch traced here: 157 us
  Pallas kernels  148 us (92%)
  local copies, waits for them, and re-layouts  8.06 us (5%)
    pallas_call x1, Pallas kernels, per_device(): pl.pallas_call(functools.partial(kernel, T, ND, frames, height, breadth,...  148 us
    unnamed x4, local copies, waits for them, and re-layouts  8.06 us

profile of v3, /device:TPU:0, one launch (start us, length us, event | category | flops | bytes accessed | tf_op | source)
XLA Modules:
  0.0 157.1 jit_solution(15271288351398425435)
XLA Ops:
  0.6 148.4 %shard_map.75 = (bf16[1024,512]{1,0:T(8,128)(2,1)}, bf16[1024,512]{1,0:T(8,128)(2,1)}, bf16[9,64,512]{2,1,0:T(8,128)(2,1)}, bf16[3,64,512]{2,1,0:T(8,128)(2,1)}) custom-call(bf16[1024,512]{1,0:T(8,128)(2,1)} %bitcast.12, bf16[1024,512]{1,0:T(8,128)(2,1)} %bitcast.13, bf16[9,1024,512]{2,1,0:T(8,128)(2,1)} %bitcast.11, bf16[3,512,1024]{2,1,0:T(8,128)(2,1)} %tw_in.1), custom_call_target="tpu_custom_call" | custom-call | flops 38654705664 | bytes 20971520 | tf_op jit(solution)/shard_map/pallas_call | solution.py:473
  149.0 2.3 %copy.12 = bf16[1,8,8,16,512]{4,3,2,1,0:T(8,128)(2,1)} copy(bf16[1,8,8,16,512]{4,3,2,1,0:T(8,128)(2,1)} %bitcast.8) | data formatting | bytes 2097152
  151.3 2.3 %copy.13 = bf16[1,8,8,16,512]{4,3,2,1,0:T(8,128)(2,1)} copy(bf16[1,8,8,16,512]{4,3,2,1,0:T(8,128)(2,1)} %bitcast.7) | data formatting | bytes 2097152
  153.6 1.9 %copy.14 = bf16[3,3,64,512]{3,2,1,0:T(8,128)(2,1)} copy(bf16[3,3,64,512]{3,2,1,0:T(8,128)(2,1)} %bitcast.9) | data formatting | bytes 1179648
  155.5 1.6 %copy.15 = bf16[3,512,64]{1,2,0:T(8,128)(2,1)} copy(bf16[3,512,64]{1,2,0:T(8,128)(2,1)} %bitcast.10) | data formatting | bytes 393216

commit v4 on v3

--- a/solution.py
+++ b/solution.py
@@ -17,14 +17,6 @@
 
 def dot(left, right, dims):
     return lax.dot_general(left, right, dims, preferred_element_type=F32)
-
-
-def bits_reversed(value, size):
-    result, step = 0, 1
-    while step < size:
-        result = result * 2 + (value // step) % 2
-        step *= 2
-    return result
 
 
 def kernel(
@@ -40,7 +32,6 @@
     POS = frames * HW
     CL = clips.shape[1]
     block = wgrad.shape[1]
-    half = frames // 2
     per_slot = CL // block
     me_t = lax.axis_index("tensor")
     me_d = lax.axis_index("dp")
@@ -163,11 +154,10 @@
     lax.fori_loop(0, frames, put_first, 0)
     pl.semaphore_wait(barrier, T - 1 + stages)
     hf_copies = []
-    for j, part in [(j, part) for part in range(2) for j in range(1, T)]:
-        some = pl.ds(part * half, frames - half if part else half)
+    for j in range(1, T):
         hf_copies.append(
-            remote(first.at[0, some, inside, :], first.at[j, some, inside, :],
-                   hf_sem.at[part, j], hf_sem.at[2 + part, j], {"tensor": peers[j]})
+            remote(first.at[0, :, inside, :], first.at[j, :, inside, :],
+                   hf_sem.at[0, j], hf_sem.at[1, j], {"tensor": peers[j]})
         )
         hf_copies[-1].start()
     for copy in og_copies:
@@ -225,10 +215,9 @@
     conv_slot(0)
     turn_first(0)
     turn_og(0)
-    for part in range(2):
-        for j in range(1, T):
-            hf_copies[part * (T - 1) + j - 1].wait_recv()
-            conv_slot(j, part * half, frames if part else half)
+    for j in range(1, T):
+        hf_copies[j - 1].wait_recv()
+        conv_slot(j)
 
     load_out = lambda f: acc[rows_of(f), :]
     center2, rate2 = statistics(load_out)
@@ -257,9 +246,6 @@
         )
         to_copies[-1].start()
 
-    for j in range(1, T):
-        turn_first(j)
-
     def back_slot(j):
         def tap(k, carry):
             rows = pl.ds(pl.multiple_of((2 - k) * HW, HW), POS)
@@ -271,18 +257,36 @@
     taps = wgrad.shape[0] + tgrad.shape[0]
     columns = (1, 0, 2)
 
+    def swapped(n):
+        return (n % 2) * (1 - (n // 2) % 2) if stages >= 3 else 0
+
+    def pick(values, s, n):
+        if stages < 3 or s not in (1, 2):
+            return values[s]
+        return values[s] + swapped(n) * (values[3 - s] - values[s])
+
+    def position(j, b, n):
+        digits = []
+        for k in range(stages):
+            low = (1 << k) < per_slot
+            digits.append((b >> k) % 2 if low else lax.rem(owners[j] // ((1 << k) // per_slot), 2))
+        place = sum(digit * (ND >> (k + 1)) for k, digit in enumerate(digits))
+        if stages >= 3:
+            place = place + swapped(n) * ((digits[2] - digits[1]) * (ND >> 3))
+        return place
+
     def source(s, n, half):
         size = ND >> (s + 1)
         rows = pl.ds(half * size, size)
         return gbuf.at[lax.rem(n, SLOTS), rows] if s == 0 else got[s - 1].at[n, rows]
 
     def exchange(s, n):
-        return remote(source(s, n, 1 - bit[s]), got[s].at[n], rs_send.at[s, n], rs_recv.at[s, n],
-                      {"dp": partner[s]})
+        return remote(source(s, n, 1 - pick(bit, s, n)), got[s].at[n], rs_send.at[s, n], rs_recv.at[s, n],
+                      {"dp": pick(partner, s, n)})
 
     def advance(s, n):
         exchange(s - 1, n).wait_recv()
-        total = got[s - 1][n].astype(F32) + source(s - 1, n, bit[s - 1])[...].astype(F32)
+        total = got[s - 1][n].astype(F32) + source(s - 1, n, pick(bit, s - 1, n))[...].astype(F32)
         if s < stages:
             got[s - 1][n] = total.astype(BF16)
             exchange(s, n).start()
@@ -299,10 +303,9 @@
             exchange(0, n - SLOTS).wait_send()
 
         for j in range(T):
-            place = bits_reversed(owners[j], T)
             product = slots(j)
             for b in range(per_slot):
-                gbuf[lax.rem(n, SLOTS), bits_reversed(b, per_slot) * T + place] = (
+                gbuf[lax.rem(n, SLOTS), position(j, b, n)] = (
                     product[b * block : (b + 1) * block].astype(BF16)
                 )
         exchange(0, n).start()
@@ -323,6 +326,8 @@
         return carry
 
     lax.fori_loop(0, 3, temporal_tap, 0)
+    for j in range(1, T):
+        turn_first(j)
 
     for j in range(1, T):
         back_slot(j)
@@ -374,10 +379,7 @@
     spatial_taps(0)
     pace(2)
     spatial_taps(1)
-    pace(4)
-    spatial_taps(2)
-    advance(1, taps - 1)
-    pace(5)
+    pace(3)
     for j in range(1, T):
         grad_slot(j)
         fsend[j - 1] = acc[...].astype(BF16)
@@ -385,7 +387,10 @@
             remote(fsend.at[j - 1], fgot.at[j - 1], gf_sem.at[0, j], gf_sem.at[1, j], {"tensor": owners[j]})
         )
         gf_copies[-1].start()
-    pace(7)
+    pace(5)
+    spatial_taps(2)
+    advance(1, taps - 1)
+    pace(6)
     grad_slot(0)
     pace(8)
     temporal(0, own)
@@ -468,7 +473,7 @@
         pltpu.VMEM((SLOTS, ND, block, CL), BF16),
     ]
     scratch += [pltpu.VMEM((taps, ND >> (s + 1), block, CL), BF16) for s in range(stages)]
-    scratch += [dma((3, T)), dma((4, T)), dma((2, T)), dma((2, T)), dma((2, T))]
+    scratch += [dma((3, T)), dma((2, T)), dma((2, T)), dma((2, T)), dma((2, T))]
     scratch += [dma((stages, taps)), dma((stages, taps))]
     mixed, clip_grad, spatial, temporal = pl.pallas_call(
         functools.partial(kernel, T, ND, frames, height, breadth, scale),

time: 160 us -> 170 us (1.062)
  Pallas kernels: 148 us -> 159 us
    pallas_call x1, Pallas kernels: 148 us -> 159 us  [per_device(): pl.pallas_call(functools.partial(kernel, T, ND, frames, height, breadth,...]
where the time goes in v4:
time: 170 us; the launch traced here: 168 us
  Pallas kernels  159 us (94%)
  local copies, waits for them, and re-layouts  8.06 us (5%)
    pallas_call x1, Pallas kernels, per_device(): pl.pallas_call(functools.partial(kernel, T, ND, frames, height, breadth,...  159 us
    unnamed x4, local copies, waits for them, and re-layouts  8.06 us

profile of v4, /device:TPU:0, one launch (start us, length us, event | category | flops | bytes accessed | tf_op | source)
XLA Modules:
  0.0 168.2 jit_solution(10760812109582781877)
XLA Ops:
  0.6 159.5 %shard_map.75 = (bf16[1024,512]{1,0:T(8,128)(2,1)}, bf16[1024,512]{1,0:T(8,128)(2,1)}, bf16[9,64,512]{2,1,0:T(8,128)(2,1)}, bf16[3,64,512]{2,1,0:T(8,128)(2,1)}) custom-call(bf16[1024,512]{1,0:T(8,128)(2,1)} %bitcast.12, bf16[1024,512]{1,0:T(8,128)(2,1)} %bitcast.13, bf16[9,1024,512]{2,1,0:T(8,128)(2,1)} %bitcast.11, bf16[3,512,1024]{2,1,0:T(8,128)(2,1)} %tw_in.1), custom_call_target="tpu_custom_call" | custom-call | flops 38654705664 | bytes 20971520 | tf_op jit(solution)/shard_map/pallas_call | solution.py:478
  160.1 2.3 %copy.12 = bf16[1,8,8,16,512]{4,3,2,1,0:T(8,128)(2,1)} copy(bf16[1,8,8,16,512]{4,3,2,1,0:T(8,128)(2,1)} %bitcast.8) | data formatting | bytes 2097152
  162.4 2.3 %copy.13 = bf16[1,8,8,16,512]{4,3,2,1,0:T(8,128)(2,1)} copy(bf16[1,8,8,16,512]{4,3,2,1,0:T(8,128)(2,1)} %bitcast.7) | data formatting | bytes 2097152
  164.7 1.9 %copy.14 = bf16[3,3,64,512]{3,2,1,0:T(8,128)(2,1)} copy(bf16[3,3,64,512]{3,2,1,0:T(8,128)(2,1)} %bitcast.9) | data formatting | bytes 1179648
  166.6 1.6 copy.15
